TPU v7x, 32 devices: a whole 2x2x4 slice. The times are simulated.
32 devices in a mesh: segment: 16 (over z, y, core), expert: 2 (over x).
Axes of the slice: x: 2, y: 2, z: 4, core: 2. Of those that a mesh axis runs over, the one named last changes fastest.
Arguments:
- grad_in: bfloat16 [256, 3072], P('expert'), may hold values from -6 to 6
- route_b: int32 [256, 2], P('expert'), may hold values from 0 to 1, as said below
- prob_b: float32 [256, 2], P('expert'), may hold values from 0.1 to 1
- pre_act: bfloat16 [2, 2, 256, 8192], P('expert', None, None, 'segment'), may hold values from -6 to 6
- saved_in: bfloat16 [256, 3072], P('expert'), may hold values from -6 to 6
- grad_saved: bfloat16 [256, 3072], P('expert'), may hold values from -4 to 4
- route_c: int32 [256, 2], P('expert'), may hold values from 0 to 1, as said below
- prob_c: float32 [256, 2], P('expert'), may hold values from 0.1 to 1
- w_gate_up: bfloat16 [2, 2, 8192, 3072], P('expert', None, 'segment'), may hold values from -0.109375 to 0.109375
- w_down: bfloat16 [2, 8192, 3072], P('expert', 'segment'), may hold values from -0.0625 to 0.0625
Outputs:
- grad_out: bfloat16 [256, 3072], P('expert')
- grad_gate_up: bfloat16 [2, 2, 8192, 3072], P('expert', None, 'segment')
- grad_down: bfloat16 [2, 8192, 3072], P('expert', 'segment')
Inputs may be any that keep to these rules, and one draw needn't show every extreme that they name: `route_b`: within each aligned block of 128 tokens the two experts of a token differ, one expert is named by exactly 128 tokens and none by more. `route_c`: within each aligned block of 128 tokens the two experts of a token differ, one expert is named by exactly 128 tokens and none by more.
All inputs are finite; a program needn't handle non-finite values.
Results may differ from a plain program's by a relative error of at most 0.0095.
Values may be sent and summed in bfloat16 or wider, within the bound.
A program may use at most 128 MiB of HBM per device.

v0:
```python
import jax
import jax.numpy as jnp
from jax import lax
from jax.sharding import PartitionSpec as P


def silu_parts(preact):
    sigmoid_val = jax.nn.sigmoid(preact)
    return (preact * sigmoid_val, sigmoid_val * (1.0 + preact * (1.0 - sigmoid_val)))


def slot_ranks(routes, experts):
    flat = routes.reshape(-1)
    onehot = (flat[:, None] == jnp.arange(experts, dtype=jnp.int32)[None, :]).astype(jnp.int32)
    before = jnp.cumsum(onehot, axis=0) - onehot
    ranks = jnp.sum(before * onehot, axis=1)
    return ranks.reshape(routes.shape[0], 2)


def slot_tables(routes, slots, probs, rows_total, per_expert):
    token_count = routes.shape[0]
    target = (routes * per_expert + slots).reshape(-1)
    slot_grid = jnp.arange(rows_total, dtype=jnp.int32)
    matches = (slot_grid[:, None] == target[None, :]).astype(jnp.int32)
    token_ids = jnp.repeat(jnp.arange(token_count, dtype=jnp.int32), 2)
    token_index = jnp.sum(matches * token_ids[None, :], axis=1)
    filled = jnp.sum(matches, axis=1).astype(jnp.float32)
    slot_scale = jnp.sum(matches.astype(jnp.float32) * probs.reshape(-1)[None, :], axis=1)
    return (token_index, filled, slot_scale)


def gather_rows(values, token_index, weight):
    picked = jnp.take(values, token_index, axis=0).astype(jnp.float32) * weight[:, None]
    return picked.astype(jnp.bfloat16)


def contract_last(left, right):
    return lax.dot_general(
        left, right, (((1,), (1,)), ((), ())), preferred_element_type=jnp.float32
    )


def contract_first(left, right):
    return lax.dot_general(
        left, right, (((0,), (0,)), ((), ())), preferred_element_type=jnp.float32
    )


def add_picked(base, returned, positions):
    summed = base.astype(jnp.float32)
    summed = summed + jnp.take(returned, positions[:, 0], axis=0).astype(jnp.float32)
    summed = summed + jnp.take(returned, positions[:, 1], axis=0).astype(jnp.float32)
    return summed.astype(jnp.bfloat16)


def body(
    grad_in, route_b, prob_b, pre_act, saved_in, grad_saved, route_c, prob_c, w_gate_up, w_down
):
    experts = lax.axis_size("expert")
    rows_total = pre_act.shape[2]
    per_expert = rows_total // experts
    model_width = grad_in.shape[1]
    hidden_units = w_down.shape[1]
    joined = w_gate_up.reshape(2 * hidden_units, model_width)
    w_last = w_down.reshape(hidden_units, model_width)
    stored = pre_act.reshape(2, rows_total, hidden_units)
    slot_b = slot_ranks(route_b, experts)
    slot_c = slot_ranks(route_c, experts)
    index_b, filled_b, scale_b = slot_tables(route_b, slot_b, prob_b, rows_total, per_expert)
    sent_b = gather_rows(grad_in, index_b, scale_b).reshape(experts, per_expert, model_width)
    index_c, filled_c, scale_c = slot_tables(route_c, slot_c, prob_c, rows_total, per_expert)
    rows_c = gather_rows(saved_in, index_c, filled_c).reshape(experts, per_expert, model_width)
    outs_c = gather_rows(grad_saved, index_c, scale_c).reshape(experts, per_expert, model_width)
    arrived_b = lax.all_to_all(sent_b, "expert", split_axis=0, concat_axis=0, tiled=True).reshape(
        rows_total, model_width
    )
    grad_act = contract_last(arrived_b, w_last)
    gate_pre = stored[0].astype(jnp.float32)
    upper_pre = stored[1].astype(jnp.float32)
    activated, slope_val = silu_parts(gate_pre)
    grad_gate = (grad_act * upper_pre * slope_val).astype(jnp.bfloat16)
    grad_up = (grad_act * activated).astype(jnp.bfloat16)
    grad_pair = jnp.concatenate([grad_gate, grad_up], axis=1)
    expert_side = jnp.dot(grad_pair, joined, preferred_element_type=jnp.float32)
    positions = route_b * per_expert + slot_b
    sections = lax.axis_size("segment")
    width_part = model_width // sections
    shares = lax.psum_scatter(
        expert_side.astype(jnp.bfloat16), "segment", scatter_dimension=1, tiled=True
    )
    returned = lax.all_to_all(
        shares.reshape(experts, per_expert, width_part),
        "expert",
        split_axis=0,
        concat_axis=0,
        tiled=True,
    )
    returned = returned.reshape(rows_total, width_part)
    start = lax.axis_index("segment") * width_part
    column_in = lax.dynamic_slice_in_dim(grad_in, start, width_part, 1)
    segment_cols = add_picked(column_in, returned, positions)
    grad_out = lax.all_gather(segment_cols, "segment", axis=1, tiled=True)
    arrived_rows, arrived_outs = (
        lax.all_to_all(rows_c, "expert", split_axis=0, concat_axis=0, tiled=True),
        lax.all_to_all(outs_c, "expert", split_axis=0, concat_axis=0, tiled=True),
    )
    sent_rows = arrived_rows.reshape(rows_total, model_width)
    out_rows = arrived_outs.reshape(rows_total, model_width)
    pre_both = contract_last(sent_rows, joined)
    gate_c = pre_both[:, :hidden_units]
    upper_c = pre_both[:, hidden_units:]
    active_c, slope_c = silu_parts(gate_c)
    hidden = (active_c * upper_c).astype(jnp.bfloat16)
    grad_act_c = contract_last(out_rows, w_last)
    grad_gate_c = (grad_act_c * upper_c * slope_c).astype(jnp.bfloat16)
    grad_up_c = (grad_act_c * active_c).astype(jnp.bfloat16)
    pair_c = jnp.concatenate([grad_gate_c, grad_up_c], axis=1)
    grad_joined = contract_first(pair_c, sent_rows).astype(jnp.bfloat16)
    grad_last = contract_first(hidden, out_rows).astype(jnp.bfloat16)
    grad_gate_up = grad_joined.reshape(1, 2, hidden_units, model_width)
    grad_down = grad_last.reshape(1, hidden_units, model_width)
    return (grad_out, grad_gate_up, grad_down)


def solution(mesh):
    in_specs = (
        P("expert", None),
        P("expert", None),
        P("expert", None),
        P("expert", None, None, "segment"),
        P("expert", None),
        P("expert", None),
        P("expert", None),
        P("expert", None),
        P("expert", None, "segment", None),
        P("expert", "segment", None),
    )
    out_specs = (
        P("expert", None),
        P("expert", None, "segment", None),
        P("expert", "segment", None),
    )
    return jax.shard_map(body, mesh=mesh, in_specs=in_specs, out_specs=out_specs, check_vma=False)
```

profile of v0, /device:TPU:0, one launch (start us, length us, event | category | flops | bytes accessed | tf_op | source)
XLA Modules:
  0.0 169.8 jit_solution(11778652042840190109)
XLA Ops:
  7.2 0.9 copy.64
  8.4 0.8 copy.72
  9.5 0.6 reduce-window.14
  10.8 0.7 multiply_add_fusion.1
  11.8 0.6 reduce-window.16
  13.1 0.7 multiply_add_fusion
  14.5 0.8 copy.68
  15.5 5.5 %gather_fusion = bf16[256,3072]{1,0:T(8,128)(2,1)} fusion(bf16[128,3072]{1,0:T(8,128)(2,1)} %param.14, s32[1024]{0:T(1024)S(1)} %pad_clamp_fusion.3), kind=kCustom, calls=%fused_computation.clone | custom fusion | bytes 3146752 | tf_op jit(solution)/shard_map/jit(_take)/gather | solution.py:33
  21.1 3.2 %multiply_convert_fusion.2 = bf16[256,3072]{1,0:T(8,128)(2,1)} fusion(bf16[256,3072]{1,0:T(8,128)(2,1)} %gather_fusion, f32[256]{0:T(256)S(1)} %multiply_reduce_fusion, pred[256]{0:T(512)(128)(4,1)S(1)} %get-tuple-element.32), kind=kLoop, calls=%fused_computation.15 | loop fusion | flops 3145728 | bytes 3147008 | tf_op jit(solution)/shard_map/convert_element_type | solution.py:34
  24.2 4.9 %all-to-all-start = ((bf16[2,128,3072]{2,1,0:T(8,128)(2,1)}), bf16[2,128,3072]{2,1,0:T(8,128)(2,1)}, u32[]{:S(2)}, u32[]{:S(2)}) async-start(bf16[2,128,3072]{2,1,0:T(8,128)(2,1)} %bitcast.86), calls=%async_computation | async-start | bytes 3145728 | tf_op jit(solution)/shard_map/all_to_all | solution.py:74
  29.6 5.5 %gather_fusion.4 = bf16[256,3072]{1,0:T(8,128)(2,1)} fusion(bf16[128,3072]{1,0:T(8,128)(2,1)} %param.18, s32[1024]{0:T(1024)S(1)} %pad_clamp_fusion), kind=kCustom, calls=%fused_computation.3.clone | custom fusion | bytes 3146752 | tf_op jit(solution)/shard_map/jit(_take)/gather | solution.py:33
  35.1 5.5 %gather_fusion.3 = bf16[256,3072]{1,0:T(8,128)(2,1)} fusion(bf16[128,3072]{1,0:T(8,128)(2,1)} %param.19, s32[1024]{0:T(1024)S(1)} %pad_clamp_fusion), kind=kCustom, calls=%fused_computation.2.clone | custom fusion | bytes 3146752 | tf_op jit(solution)/shard_map/jit(_take)/gather | solution.py:33
  40.7 4.9 %multiply_convert_fusion.1 = (bf16[256,3072]{1,0:T(8,128)(2,1)}, bf16[256,3072]{1,0:T(8,128)(2,1)}) fusion(bf16[256,3072]{1,0:T(8,128)(2,1)} %gather_fusion.3, f32[256]{0:T(256)S(1)} %fusion.22, pred[256]{0:T(512)(128)(4,1)S(1)} %get-tuple-element.31, f32[256]{0:T(256)S(1)} %convert_element_type.123, bf16[256,3072]{1,0:T(8,128)(2,1)} %gather_fusion.4), kind=kLoop, calls=%fused_computation.14 | loop fusion | flops 6291456 | bytes 6293760 | tf_op jit(solution)/shard_map/convert_element_type | solution.py:34
  45.6 4.4 %all-to-all-done = bf16[2,128,3072]{2,1,0:T(8,128)(2,1)} async-done(((bf16[2,128,3072]{2,1,0:T(8,128)(2,1)}), bf16[2,128,3072]{2,1,0:T(8,128)(2,1)}, u32[]{:S(2)}, u32[]{:S(2)}) %all-to-all-start) | async-done | bytes 1572896 | tf_op jit(solution)/shard_map/all_to_all | solution.py:74
  50.0 4.6 %all-to-all-start.3 = ((bf16[2,128,3072]{2,1,0:T(8,128)(2,1)}), bf16[2,128,3072]{2,1,0:T(8,128)(2,1)}, u32[]{:S(2)}, u32[]{:S(2)}) async-start(bf16[2,128,3072]{2,1,0:T(8,128)(2,1)} %bitcast.88), calls=%async_computation.4 | async-start | bytes 3145728 | tf_op jit(solution)/shard_map/all_to_all | solution.py:104
  54.6 2.7 %fusion.11 = (bf16[256,512]{1,0:T(8,128)(2,1)S(1)}, bf16[256,512]{1,0:T(8,128)(2,1)S(1)}) fusion(bf16[1,2,256,512]{3,2,1,0:T(8,128)(2,1)} %param.17, bf16[256,3072]{1,0:T(8,128)(2,1)} %bitcast.3, bf16[1,512,3072]{2,1,0:T(8,128)(2,1)S(1)} %copy-done), kind=kOutput, calls=%fused_computation.25 | convolution fusion | flops 807272448 | bytes 5767168 | tf_op jit(solution)/shard_map/dot_general | solution.py:38
  57.3 6.5 %convolution_convert_fusion.2 = bf16[256,3072]{0,1:T(8,128)(2,1)} fusion(bf16[1024,3072]{1,0:T(8,128)(2,1)} %bitcast.91, bf16[256,512]{1,0:T(8,128)(2,1)S(1)} %get-tuple-element.24, bf16[256,512]{1,0:T(8,128)(2,1)S(1)} %get-tuple-element.23), kind=kOutput, calls=%fused_computation.8 | convolution fusion | flops 1612447744 | bytes 8388608 | tf_op jit(solution)/shard_map/dot_general | solution.py:84
  63.9 9.7 %all-to-all-done.3 = bf16[2,128,3072]{2,1,0:T(8,128)(2,1)} async-done(((bf16[2,128,3072]{2,1,0:T(8,128)(2,1)}), bf16[2,128,3072]{2,1,0:T(8,128)(2,1)}, u32[]{:S(2)}, u32[]{:S(2)}) %all-to-all-start.3) | async-done | bytes 1572896 | tf_op jit(solution)/shard_map/all_to_all | solution.py:104
  73.6 4.9 %all-to-all-start.2 = ((bf16[2,128,3072]{2,1,0:T(8,128)(2,1)}), bf16[2,128,3072]{2,1,0:T(8,128)(2,1)}, u32[]{:S(2)}, u32[]{:S(2)}) async-start(bf16[2,128,3072]{2,1,0:T(8,128)(2,1)} %bitcast.87), calls=%async_computation.3 | async-start | bytes 3145728 | tf_op jit(solution)/shard_map/all_to_all | solution.py:105
  78.5 6.2 %fusion.33 = f32[256,1024]{1,0:T(8,128)} fusion(bf16[256,3072]{1,0:T(8,128)(2,1)} %bitcast.15, bf16[1024,3072]{1,0:T(8,128)(2,1)} %bitcast.92), kind=kOutput, calls=%fused_computation.82 | convolution fusion | flops 1610612736 | bytes 8912896 | tf_op jit(solution)/shard_map/dot_general | solution.py:38
  84.7 11.6 %all-to-all-done.2 = bf16[2,128,3072]{2,1,0:T(8,128)(2,1)} async-done(((bf16[2,128,3072]{2,1,0:T(8,128)(2,1)}), bf16[2,128,3072]{2,1,0:T(8,128)(2,1)}, u32[]{:S(2)}, u32[]{:S(2)}) %all-to-all-start.2) | async-done | bytes 1572896 | tf_op jit(solution)/shard_map/all_to_all | solution.py:105
  96.3 2.8 %multiply_convert_fusion.5 = (bf16[256,512]{1,0:T(8,128)(2,1)S(1)}, bf16[256,512]{1,0:T(8,128)(2,1)S(1)}) fusion(f32[256,1024]{1,0:T(8,128)} %fusion.33, bf16[256,3072]{1,0:T(8,128)(2,1)} %bitcast.13, bf16[1,512,3072]{2,1,0:T(8,128)(2,1)S(1)} %copy-done), kind=kOutput, calls=%fused_computation.37 | convolution fusion | flops 807010304 | bytes 6291456 | tf_op jit(solution)/shard_map/dot_general | solution.py:38
  99.1 6.0 %convolution_convert_fusion = bf16[1024,3072]{1,0:T(8,128)(2,1)} fusion(bf16[256,3072]{1,0:T(8,128)(2,1)} %bitcast.15, bf16[256,512]{1,0:T(8,128)(2,1)S(1)} %get-tuple-element.22, bf16[256,512]{1,0:T(8,128)(2,1)S(1)} %get-tuple-element.21), kind=kOutput, calls=%fused_computation.5 | convolution fusion | flops 1614807040 | bytes 8388608 | tf_op jit(solution)/shard_map/dot_general | solution.py:44
  105.1 20.2 %reduce-scatter.2.cloned.1.call-done = bf16[256,192]{0,1:T(8,128)(2,1)} async-done(((bf16[256,3072]{0,1:T(8,128)(2,1)}), bf16[256,192]{0,1:T(8,128)(2,1)}) %reduce-scatter.2.cloned.1.call-update) | async-done | bytes 98320 | tf_op jit(solution)/shard_map/reduce_scatter | solution.py:88
  125.3 1.5 copy_bitcast_fusion
  126.8 3.3 %all-to-all-start.1 = ((bf16[2,128,192]{1,2,0:T(8,128)(2,1)}), bf16[2,128,192]{1,2,0:T(8,128)(2,1)S(1)}, u32[]{:S(2)}, u32[]{:S(2)}) async-start(bf16[2,128,192]{1,2,0:T(8,128)(2,1)} %copy_bitcast_fusion), calls=%async_computation.2 | async-start | bytes 196608 | tf_op jit(solution)/shard_map/all_to_all | solution.py:91
  130.2 4.5 %fusion = bf16[1,512,3072]{2,1,0:T(8,128)(2,1)} fusion(bf16[256,3072]{1,0:T(8,128)(2,1)} %bitcast.13, f32[256,1024]{1,0:T(8,128)} %fusion.33), kind=kOutput, calls=%fused_computation.7 | convolution fusion | flops 807665664 | bytes 5767168 | tf_op jit(solution)/shard_map/dot_general | solution.py:44
  134.8 0.8 gather_fusion.2
  135.6 0.8 gather_fusion.1
  136.5 1.0 add_convert_fusion
  137.6 23.0 %all_gather.3 = bf16[128,3072]{0,1:T(8,128)(2,1)} all-gather(bf16[128,192]{0,1:T(8,128)(2,1)S(1)} %copy.71), channel_id=1, replica_groups=mesh['segment'=16,'expert'=2] {'segment'}, dimensions={1}, use_global_device_ids=true | all-gather | bytes 835584 | tf_op jit(solution)/shard_map/all_gather | solution.py:102
  160.6 2.3 %copy.77 = bf16[128,3072]{1,0:T(8,128)(2,1)} copy(bf16[128,3072]{0,1:T(8,128)(2,1)} %all_gather.3) | data formatting | bytes 1572864
  (46 shorter events, 3.8 us)
Async XLA Ops:
  7.2 47.4 %copy-start = (bf16[1,512,3072]{2,1,0:T(8,128)(2,1)S(1)}, bf16[1,512,3072]{2,1,0:T(8,128)(2,1)}, u32[]{:S(2)}) copy-start(bf16[1,512,3072]{2,1,0:T(8,128)(2,1)} %param.23) | copy-start | bytes 9437188
  24.2 4.9 %copy-start.1 = (f32[128,2]{0,1:T(2,128)S(1)}, f32[128,2]{0,1:T(2,128)}, u32[]{:S(2)}) copy-start(f32[128,2]{0,1:T(2,128)} %param.21) | copy-start | bytes 3076
  24.2 25.7 %all-to-all-start = ((bf16[2,128,3072]{2,1,0:T(8,128)(2,1)}), bf16[2,128,3072]{2,1,0:T(8,128)(2,1)}, u32[]{:S(2)}, u32[]{:S(2)}) async-start(bf16[2,128,3072]{2,1,0:T(8,128)(2,1)} %bitcast.86), calls=%async_computation | async-start | bytes 3145728 | tf_op jit(solution)/shard_map/all_to_all | solution.py:74
  50.0 23.6 %all-to-all-start.3 = ((bf16[2,128,3072]{2,1,0:T(8,128)(2,1)}), bf16[2,128,3072]{2,1,0:T(8,128)(2,1)}, u32[]{:S(2)}, u32[]{:S(2)}) async-start(bf16[2,128,3072]{2,1,0:T(8,128)(2,1)} %bitcast.88), calls=%async_computation.4 | async-start | bytes 3145728 | tf_op jit(solution)/shard_map/all_to_all | solution.py:104
  54.6 70.7 %reduce-scatter.2.cloned.1.call-start = ((), (), s32[]{:S(2)}) async-start(), calls=%async_computation.5 | async-start | bytes 1671168 | tf_op jit(solution)/shard_map/reduce_scatter | solution.py:88
  73.6 22.7 %all-to-all-start.2 = ((bf16[2,128,3072]{2,1,0:T(8,128)(2,1)}), bf16[2,128,3072]{2,1,0:T(8,128)(2,1)}, u32[]{:S(2)}, u32[]{:S(2)}) async-start(bf16[2,128,3072]{2,1,0:T(8,128)(2,1)} %bitcast.87), calls=%async_computation.3 | async-start | bytes 3145728 | tf_op jit(solution)/shard_map/all_to_all | solution.py:105
  126.8 7.8 %all-to-all-start.1 = ((bf16[2,128,192]{1,2,0:T(8,128)(2,1)}), bf16[2,128,192]{1,2,0:T(8,128)(2,1)S(1)}, u32[]{:S(2)}, u32[]{:S(2)}) async-start(bf16[2,128,192]{1,2,0:T(8,128)(2,1)} %copy_bitcast_fusion), calls=%async_computation.2 | async-start | bytes 196608 | tf_op jit(solution)/shard_map/all_to_all | solution.py:91
Sparse Core Ops, SparseCore 0:
  64.0 61.2 reduce-scatter.1
where the time goes:
time: 171 us; the launch traced here: 170 us
  waiting for transfers between devices  45.9 us (27%)
  matrix products  28.7 us (17%)
  local copies, waits for them, and re-layouts  27.3 us (16%)
  blocking collectives  23 us (13%)
  starting transfers between devices  17.8 us (10%)
  between operations  14.3 us (8%)
  other arithmetic  12.8 us (7%)
    all_gather x1, blocking collectives, body(): grad_out = lax.all_gather(segment_cols, 'segment', axis=1, tiled=True)  23 us
    reduce_scatter x1, waiting for transfers between devices, body(): lax.psum_scatter(expert_side.astype(jnp.bfloat16), 'segment', scatter_dim...  20.2 us
    gather x3, local copies, waits for them, and re-layouts, gather_rows(): jnp.take(values, token_index, axis=0).astype(jnp.float32) * weight[:, None]  16.6 us
    dot_general x3, matrix products, contract_last(): lax.dot_general(left, right, (((1,), (1,)), ((), ())), preferred_element_...  11.7 us
    all_to_all x1, waiting for transfers between devices, body(): lax.all_to_all(outs_c, 'expert', split_axis=0, concat_axis=0, tiled=True)  11.6 us
    dot_general x2, matrix products, contract_first(): lax.dot_general(left, right, (((0,), (0,)), ((), ())), preferred_element_...  10.4 us
    all_to_all x1, waiting for transfers between devices, body(): lax.all_to_all(rows_c, 'expert', split_axis=0, concat_axis=0, tiled=True)  9.73 us
    convert_element_type x2, other arithmetic, gather_rows(): return picked.astype(jnp.bfloat16)  8.1 us
  transfers between devices with their start and end apart: 5, of which 4 were waited for; matrix products, arithmetic and copies ran while one was open for 27% of the time, Pallas kernels for 0%

commit v1 on v0

--- a/solution.py
+++ b/solution.py
@@ -1,6 +1,10 @@
+import functools
+
 import jax
 import jax.numpy as jnp
 from jax import lax
+from jax.experimental import pallas as pl
+from jax.experimental.pallas import tpu as pltpu
 from jax.sharding import PartitionSpec as P
 
 
@@ -122,6 +126,349 @@
     return (grad_out, grad_gate_up, grad_down)
 
 
+MESH = pl.DeviceIdType.MESH
+BF16 = jnp.bfloat16
+F32 = jnp.float32
+
+
+def exchange_kernel(
+    zn, gin, sin, gsv, rb, pb, rc, pc, pre, wgu, wd,
+    gout, rows_o, outs_o, gt_o,
+    tok, wv, prev, wsend, wrecv, ps, pr, pf, pm, r2a, r2b, s3a, s3b, r3a, r3b, qf, qs, r4, go, gt,
+    send_sem, recv_sem, local_sem,
+):
+    s = lax.axis_index("segment")
+    x = lax.axis_index("expert")
+    c, y, z = s % 2, (s // 2) % 2, s // 4
+    T, D = gin.shape
+    H = wd.shape[0]
+    half, part = D // 2, D // 4
+    yrows, zrows, quarter = T // 2, T // 2 // zn, T // 4
+    piece = quarter // 2
+    sib = {"segment": s + 1 - 2 * c, "expert": x}
+    ypal = {"segment": s + 2 - 4 * y, "expert": x}
+    xpal = {"segment": s, "expert": 1 - x}
+    zpal = [None] + [{"segment": ((z + k) % zn) * 4 + s % 4, "expert": x} for k in range(1, zn)]
+
+    used = [0, 0]
+    sent = []
+
+    def remote(src, dst, to):
+        i = used[0]
+        used[0] += 1
+        return pltpu.make_async_remote_copy(
+            src_ref=src, dst_ref=dst, send_sem=send_sem.at[i], recv_sem=recv_sem.at[i],
+            device_id=to, device_id_type=MESH,
+        )
+
+    def start(copy):
+        copy.start()
+        sent.append(copy)
+        return copy
+
+    def local(src, dst):
+        i = used[1]
+        used[1] += 1
+        copy = pltpu.make_async_copy(src, dst, local_sem.at[i])
+        copy.start()
+        return copy
+
+    in_b = local(gin, tok.at[0, pl.ds(0, T)])
+    in_wd = local(wd, wv.at[pl.ds(2 * H, H)])
+    in_pre = local(pre, prev)
+    in_wgu = local(wgu, wv.at[pl.ds(0, 2 * H)])
+    in_rows = local(sin, tok.at[1, pl.ds(0, T)])
+    in_outs = local(gsv, tok.at[2, pl.ds(0, T)])
+
+    barrier = pltpu.get_barrier_semaphore()
+    pals = [sib, ypal, xpal] + zpal[1:]
+    for pal in pals:
+        pl.semaphore_signal(barrier, inc=1, device_id=pal, device_id_type=MESH)
+    pl.semaphore_wait(barrier, len(pals))
+
+    def at_rows(a, q, h, base):
+        return tok.at[a, pl.ds(pl.multiple_of(base + q * quarter + h * piece, 16), piece)]
+
+    q_me = 2 * y + c
+    q_y = 2 * (1 - y) + c
+    arrays = (gin, sin, gsv)
+    by_x, by_y, by_sib = {}, {}, {}
+    for a in range(3):
+        for h in range(2):
+            src = arrays[a].at[pl.ds(pl.multiple_of(q_me * quarter + h * piece, 16), piece)]
+            by_x[a, h] = remote(src, at_rows(a, q_me, h, T), xpal)
+            by_y[a, h] = remote(at_rows(a, q_me, h, T), at_rows(a, q_me, h, T), ypal)
+            by_sib[a, h, 0] = remote(at_rows(a, q_me, h, T), at_rows(a, q_me, h, T), sib)
+            by_sib[a, h, 1] = remote(at_rows(a, q_y, h, T), at_rows(a, q_y, h, T), sib)
+
+    def send_x(a):
+        for h in range(2):
+            start(by_x[a, h])
+
+    def pass_x(a):
+        for h in range(2):
+            by_x[a, h].wait_recv()
+            start(by_y[a, h])
+            start(by_sib[a, h, 0])
+
+    def pass_y(a):
+        for h in range(2):
+            by_y[a, h].wait_recv()
+            start(by_sib[a, h, 1])
+
+    def wait_sib(a):
+        for h in range(2):
+            for i in range(2):
+                by_sib[a, h, i].wait_recv()
+
+    send_x(0)
+
+    def share(routes, probs, expert):
+        picked = jnp.where(routes[...] == expert, probs[...], 0.0)
+        return picked[0:1] + picked[1:2]
+
+    wsend[...] = jnp.zeros_like(wsend)
+    wsend[0:1, :] = share(rb, pb, 1 - x)
+    wsend[1:2, :] = share(rc, pc, 1 - x)
+    weights = start(remote(wsend, wrecv, xpal))
+
+    def nt(left, right):
+        return lax.dot_general(left, right, (((1,), (1,)), ((), ())), preferred_element_type=F32)
+
+    def column(row):
+        return jnp.broadcast_to(row, (T, T)).T[:, 0:1]
+
+    def hidden_b(first, scale, block):
+        act = nt(tok[0, first:first + T, :], wv[2 * H:3 * H, :]) * scale
+        rows = pl.ds(pl.multiple_of(block * T, T), T)
+        gate = prev[0, rows, :].astype(F32)
+        upper = prev[1, rows, :].astype(F32)
+        activated, slope = silu_parts(gate)
+        return (act * upper * slope).astype(BF16), (act * activated).astype(BF16)
+
+    tile = part
+
+    def back_b(pair, first, core, put):
+        for n in range(half // tile):
+            cols = pl.ds(pl.multiple_of(core * half + n * tile, 128), tile)
+            total = jnp.dot(pair[0], wv[0:H, cols], preferred_element_type=F32)
+            total = total + jnp.dot(pair[1], wv[H:2 * H, cols], preferred_element_type=F32)
+            put(slice(first, first + T), slice(n * tile, n * tile + tile), total)
+
+    def put_send(rows, cols, total):
+        ps[rows, cols] = total.astype(BF16)
+
+    def put_keep(rows, cols, total):
+        pf[rows, cols] = total
+
+    in_b.wait()
+    in_wd.wait()
+    in_pre.wait()
+    pair_own = hidden_b(0, column(share(rb, pb, x)), x)
+    pass_x(0)
+    send_x(1)
+    in_wgu.wait()
+    back_b(pair_own, 0, 1 - c, put_send)
+    to_sib = [remote(ps.at[pl.ds(i * T, T)], pr.at[pl.ds(i * T, T)], sib) for i in range(2)]
+    start(to_sib[0])
+    pass_y(0)
+    back_b(pair_own, 0, c, put_keep)
+    weights.wait_recv()
+    wait_sib(0)
+    pair_other = hidden_b(T, column(wrecv[0:1, :]), 1 - x)
+    back_b(pair_other, T, 1 - c, put_send)
+    start(to_sib[1])
+    pass_x(1)
+    back_b(pair_other, T, c, put_keep)
+
+    mine = pl.multiple_of(y * yrows, 16)
+    theirs = pl.multiple_of((1 - y) * yrows, 16)
+    lo, hi = slice(0, part), slice(part, half)
+    to_sib[0].wait_recv()
+    pf[0:T, :] = pf[0:T, :] + pr[0:T, :].astype(F32)
+    pm[0:T, :] = pf[0:T, :].astype(BF16)
+    s2b0 = start(remote(pm.at[pl.ds(theirs, yrows), pl.ds(part, part)], r2b.at[pl.ds(0, yrows)], ypal))
+    to_sib[1].wait_recv()
+    pf[T:2 * T, :] = pf[T:2 * T, :] + pr[T:2 * T, :].astype(F32)
+    pm[T:2 * T, :] = pf[T:2 * T, :].astype(BF16)
+    s2a = start(remote(pm.at[pl.ds(T, T), pl.ds(0, part)], r2a, xpal))
+    s2b1 = start(remote(pm.at[pl.ds(T + theirs, yrows), pl.ds(part, part)], r2b.at[pl.ds(yrows, yrows)], ypal))
+
+    pass_y(1)
+    in_rows.wait()
+    wait_sib(1)
+    out_rows = local(tok.at[1], rows_o)
+    for i in range(2 * H // 256):
+        units = slice(i * 256, i * 256 + 256)
+        gt[units, :] = nt(wv[units, :], tok[1])
+
+    s2a.wait_recv()
+    s3a[...] = (pf[pl.ds(theirs, yrows), lo] + r2a[pl.ds(theirs, yrows), :].astype(F32)).astype(BF16)
+    c3a = start(remote(s3a, r3a, ypal))
+    s2b1.wait_recv()
+    s3b[...] = (pf[pl.ds(T + mine, yrows), hi] + r2b[yrows:2 * yrows, :].astype(F32)).astype(BF16)
+    c3b = start(remote(s3b, r3b, xpal))
+    s2b0.wait_recv()
+    qf[:, lo] = pf[pl.ds(mine, yrows), lo] + r2a[pl.ds(mine, yrows), :].astype(F32)
+    qf[:, hi] = pf[pl.ds(mine, yrows), hi] + r2b[0:yrows, :].astype(F32)
+    c3a.wait_recv()
+    qf[:, lo] = qf[:, lo] + r3a[...].astype(F32)
+    c3b.wait_recv()
+    qf[:, hi] = qf[:, hi] + r3b[...].astype(F32)
+    qs[...] = qf[...].astype(BF16)
+    z_sums = []
+    for k in range(1, zn):
+        there = pl.ds(pl.multiple_of(((z + k) % zn) * zrows, 16), zrows)
+        z_sums.append(start(remote(qs.at[there], r4.at[k - 1], zpal[k])))
+    send_x(2)
+    here = pl.multiple_of(z * zrows, 16)
+    cols_me = pl.ds(pl.multiple_of(c * half, 128), half)
+    chunk = qf[pl.ds(here, zrows), :] + tok[0, pl.ds(mine + here, zrows), cols_me].astype(F32)
+    for k in range(1, zn):
+        z_sums[k - 1].wait_recv()
+        chunk = chunk + r4[k - 1].astype(F32)
+    go[pl.ds(mine + here, zrows), cols_me] = chunk.astype(BF16)
+
+    def finished(yy, k):
+        return go.at[pl.ds(pl.multiple_of(yy * yrows + ((z + zn - k) % zn) * zrows, 16), zrows), cols_me]
+
+    z_out = [None] + [start(remote(finished(y, 0), finished(y, 0), zpal[k])) for k in range(1, zn)]
+    y_out, sib_out = [], []
+    y_out.append(start(remote(finished(y, 0), finished(y, 0), ypal)))
+    sib_out.append(start(remote(finished(y, 0), finished(y, 0), sib)))
+    pass_x(2)
+    for k in range(1, zn):
+        z_out[k].wait_recv()
+        y_out.append(start(remote(finished(y, k), finished(y, k), ypal)))
+        sib_out.append(start(remote(finished(y, k), finished(y, k), sib)))
+    pass_y(2)
+    in_outs.wait()
+    wait_sib(2)
+    out_outs = local(tok.at[2], outs_o)
+    scale_own = share(rc, pc, x)
+    scale_c = jnp.concatenate([scale_own, wrecv[1:2, :]], axis=1)
+    gtb = gt_o
+    for i in range(H // 256):
+        units = slice(i * 256, i * 256 + 256)
+        uppers = slice(H + i * 256, H + i * 256 + 256)
+        downs = slice(2 * H + i * 256, 2 * H + i * 256 + 256)
+        act = nt(wv[downs, :], tok[2]) * scale_c
+        upper = gt[uppers, :]
+        activated, slope = silu_parts(gt[units, :])
+        gtb[units, :] = (act * upper * slope).astype(BF16)
+        gtb[uppers, :] = (act * activated).astype(BF16)
+        gtb[downs, :] = (activated * upper * scale_c).astype(BF16)
+    for k in range(zn):
+        y_out[k].wait_recv()
+        sib_out.append(start(remote(finished(1 - y, k), finished(1 - y, k), sib)))
+    for copy in sib_out:
+        copy.wait_recv()
+    out_go = local(go, gout)
+    for copy in sent:
+        copy.wait_send()
+    out_rows.wait()
+    out_outs.wait()
+    out_go.wait()
+
+
+def weight_kernel(joined_steps, gt, rows, outs, gin, joint, last, gout):
+    i = pl.program_id(0)
+
+    @pl.when(i == 0)
+    def _():
+        gout[...] = gin[...]
+
+    @pl.when(i < joined_steps)
+    def _():
+        joint[...] = jnp.dot(gt[...], rows[...], preferred_element_type=F32).astype(BF16)
+
+    @pl.when(i >= joined_steps)
+    def _():
+        last[...] = jnp.dot(gt[...], outs[...], preferred_element_type=F32).astype(BF16)
+
+
+def dense_body(
+    grad_in, route_b, prob_b, pre_act, saved_in, grad_saved, route_c, prob_c, w_gate_up, w_down
+):
+    sections = lax.axis_size("segment")
+    zn = sections // 4
+    T, D = grad_in.shape
+    H = w_down.shape[1]
+    half, part = D // 2, D // 4
+    copies = 24 + 1 + 2 + 3 + 2 + 2 * (zn - 1) + 3 * zn
+    hbm = pl.BlockSpec(memory_space=pl.ANY)
+    vmem = pl.BlockSpec(memory_space=pltpu.VMEM)
+    gout, rows, outs, gt = pl.pallas_call(
+        functools.partial(exchange_kernel, zn),
+        out_shape=(
+            jax.ShapeDtypeStruct((T, D), BF16),
+            jax.ShapeDtypeStruct((2 * T, D), BF16),
+            jax.ShapeDtypeStruct((2 * T, D), BF16),
+            jax.ShapeDtypeStruct((3 * H, 2 * T), BF16),
+        ),
+        in_specs=[hbm] * 3 + [vmem] * 4 + [hbm] * 3,
+        out_specs=(hbm, hbm, hbm, vmem),
+        scratch_shapes=[
+            pltpu.VMEM((3, 2 * T, D), BF16),
+            pltpu.VMEM((3 * H, D), BF16),
+            pltpu.VMEM((2, 2 * T, H), BF16),
+            pltpu.VMEM((8, T), F32),
+            pltpu.VMEM((8, T), F32),
+            pltpu.VMEM((2 * T, half), BF16),
+            pltpu.VMEM((2 * T, half), BF16),
+            pltpu.VMEM((2 * T, half), F32),
+            pltpu.VMEM((2 * T, half), BF16),
+            pltpu.VMEM((T, part), BF16),
+            pltpu.VMEM((T, part), BF16),
+            pltpu.VMEM((T // 2, part), BF16),
+            pltpu.VMEM((T // 2, part), BF16),
+            pltpu.VMEM((T // 2, part), BF16),
+            pltpu.VMEM((T // 2, part), BF16),
+            pltpu.VMEM((T // 2, half), F32),
+            pltpu.VMEM((T // 2, half), BF16),
+            pltpu.VMEM((zn - 1, T // 2 // zn, half), BF16),
+            pltpu.VMEM((T, D), BF16),
+            pltpu.VMEM((2 * H, 2 * T), F32),
+            pltpu.SemaphoreType.DMA((copies,)),
+            pltpu.SemaphoreType.DMA((copies,)),
+            pltpu.SemaphoreType.DMA((9,)),
+        ],
+        compiler_params=pltpu.CompilerParams(
+            collective_id=0, has_side_effects=True, vmem_limit_bytes=56 * 1024 * 1024
+        ),
+        name="exchange",
+    )(
+        grad_in, saved_in, grad_saved, route_b.T, prob_b.T, route_c.T, prob_c.T,
+        pre_act.reshape(2, 2 * T, H), w_gate_up.reshape(2 * H, D), w_down.reshape(H, D),
+    )
+    rows_step = 256
+    joined_steps, last_steps = 2 * H // rows_step, H // rows_step
+    whole = pl.BlockSpec((2 * T, D), lambda i: (0, 0))
+    one = pl.BlockSpec((T, D), lambda i: (0, 0))
+    joint, last, grad_out = pl.pallas_call(
+        functools.partial(weight_kernel, joined_steps),
+        grid=(joined_steps + last_steps,),
+        out_shape=(
+            jax.ShapeDtypeStruct((2 * H, D), BF16),
+            jax.ShapeDtypeStruct((H, D), BF16),
+            jax.ShapeDtypeStruct((T, D), BF16),
+        ),
+        in_specs=[pl.BlockSpec((rows_step, 2 * T), lambda i: (i, 0)), whole, whole, one],
+        out_specs=(
+            pl.BlockSpec((rows_step, D), lambda i: (jnp.minimum(i, joined_steps - 1), 0)),
+            pl.BlockSpec((rows_step, D), lambda i: (jnp.maximum(i - joined_steps, 0), 0)),
+            one,
+        ),
+        compiler_params=pltpu.CompilerParams(vmem_limit_bytes=48 * 1024 * 1024),
+        name="weights",
+    )(gt, rows, outs, gout)
+    return grad_out, joint.reshape(1, 2, H, D), last.reshape(1, H, D)
+
+
+def dense_fits(mesh):
+    return mesh.shape["expert"] == 2 and mesh.shape["segment"] == 16
+
+
 def solution(mesh):
     in_specs = (
         P("expert", None),
@@ -140,4 +487,5 @@
         P("expert", None, "segment", None),
         P("expert", "segment", None),
     )
-    return jax.shard_map(body, mesh=mesh, in_specs=in_specs, out_specs=out_specs, check_vma=False)
+    chosen = dense_body if dense_fits(mesh) else body
+    return jax.shard_map(chosen, mesh=mesh, in_specs=in_specs, out_specs=out_specs, check_vma=False)

time: 171 us -> 64.8 us (0.38)
  Pallas kernels: 0 us -> 58.8 us
  waiting for transfers between devices: 45.9 us -> 0 us
  matrix products: 28.7 us -> 0 us
  blocking collectives: 23 us -> 0 us
  local copies, waits for them, and re-layouts: 27.3 us -> 5.07 us
  starting transfers between devices: 17.8 us -> 0 us
  between operations: 14.3 us -> 0.65 us
  other arithmetic: 12.8 us -> 0 us
    pallas_call x0 -> x2, Pallas kernels: none -> 58.8 us  [the longest x1 52.2 us: dense_body(): pl.pallas_call(functools.partial(exchange_kernel, zn), out_shape=(jax.Sha...]
    dot_general x6 -> x0, matrix products: 28.7 us -> none  [the longest x3 11.7 us: contract_last(): lax.dot_general(left, right, (((1,), (1,)), ((), ())), preferred_element_...]
    all_to_all x4 -> x0, waiting for transfers between devices: 25.7 us -> none  [the longest x1 11.6 us: body(): lax.all_to_all(outs_c, 'expert', split_axis=0, concat_axis=0, tiled=True)]
    all_gather x1 -> x0, blocking collectives: 23 us -> none  [body(): grad_out = lax.all_gather(segment_cols, 'segment', axis=1, tiled=True)]
    reduce_scatter x1 -> x0, waiting for transfers between devices: 20.2 us -> none  [body(): lax.psum_scatter(expert_side.astype(jnp.bfloat16), 'segment', scatter_dim...]
    gather x5 -> x0, local copies, waits for them, and re-layouts: 18.3 us -> none  [the longest x3 16.6 us: gather_rows(): jnp.take(values, token_index, axis=0).astype(jnp.float32) * weight[:, None]]
    all_to_all x4 -> x0, starting transfers between devices: 17.7 us -> none  [the longest x1 4.92 us: body(): lax.all_to_all(sent_b, 'expert', split_axis=0, concat_axis=0, tiled=True)]
    convert_element_type x6 -> x0, other arithmetic: 9.14 us -> none  [the longest x2 8.1 us: gather_rows(): return picked.astype(jnp.bfloat16)]
  transfers between devices with their start and end apart: 5 -> 0, of which waited for: 4 -> 0; matrix products, arithmetic and copies ran while one was open for 27% -> 0% of each run, Pallas kernels for 0% -> 0%
where the time goes in v1:
time: 64.8 us; the launch traced here: 64.5 us
  Pallas kernels  58.8 us (91%)
  local copies, waits for them, and re-layouts  5.07 us (8%)
  between operations  0.65 us (1%)
    pallas_call x1, Pallas kernels, dense_body(): pl.pallas_call(functools.partial(exchange_kernel, zn), out_shape=(jax.Sha...  52.2 us
    pallas_call x1, Pallas kernels, dense_body(): pl.pallas_call(functools.partial(weight_kernel, joined_steps), grid=(join...  6.61 us
    unnamed x8, local copies, waits for them, and re-layouts  5.07 us

profile of v1, /device:TPU:0, one launch (start us, length us, event | category | flops | bytes accessed | tf_op | source)
XLA Modules:
  0.0 64.5 jit_solution(8811890783671683968)
XLA Ops:
  0.6 52.2 %exchange.1 = (bf16[128,3072]{1,0:T(8,128)(2,1)}, bf16[256,3072]{1,0:T(8,128)(2,1)}, bf16[256,3072]{1,0:T(8,128)(2,1)}, bf16[1536,256]{1,0:T(8,128)(2,1)}) custom-call(bf16[128,3072]{1,0:T(8,128)(2,1)} %gin.1, bf16[128,3072]{1,0:T(8,128)(2,1)} %sin.1, bf16[128,3072]{1,0:T(8,128)(2,1)} %gsv.1, s32[2,128]{1,0:T(2,128)} %bitcast.12, f32[2,128]{1,0:T(2,128)} %bitcast.13, ...), custom_call_target="tpu_custom_call" | custom-call | tf_op jit(solution)/shard_map/exchange/pallas_call | solution.py:401
  52.8 0.0 copy-start
  52.8 1.4 %copy-done = bf16[256,3072]{1,0:T(8,128)(2,1)S(1)} copy-done((bf16[256,3072]{1,0:T(8,128)(2,1)S(1)}, bf16[256,3072]{1,0:T(8,128)(2,1)}, u32[]{:S(2)}) %copy-start) | copy-done | bytes 1572888
  54.2 0.0 copy-start.1
  54.2 1.4 %copy-done.1 = bf16[256,3072]{1,0:T(8,128)(2,1)S(1)} copy-done((bf16[256,3072]{1,0:T(8,128)(2,1)S(1)}, bf16[256,3072]{1,0:T(8,128)(2,1)}, u32[]{:S(2)}) %copy-start.1) | copy-done | bytes 1572888
  55.6 0.0 copy-start.2
  55.6 1.1 %copy-done.2 = bf16[128,3072]{1,0:T(8,128)(2,1)S(1)} copy-done((bf16[128,3072]{1,0:T(8,128)(2,1)S(1)}, bf16[128,3072]{1,0:T(8,128)(2,1)}, u32[]{:S(2)}) %copy-start.2) | copy-done | bytes 786456
  56.8 0.0 copy-start.3
  56.8 1.1 %copy-done.3 = bf16[1536,256]{1,0:T(8,128)(2,1)S(1)} copy-done((bf16[1536,256]{1,0:T(8,128)(2,1)S(1)}, bf16[1536,256]{1,0:T(8,128)(2,1)}, u32[]{:S(2)}) %copy-start.3) | copy-done | bytes 786456
  57.9 6.6 %weights.1 = (bf16[1024,3072]{1,0:T(8,128)(2,1)}, bf16[512,3072]{1,0:T(8,128)(2,1)}, bf16[128,3072]{1,0:T(8,128)(2,1)}) custom-call(bf16[1536,256]{1,0:T(8,128)(2,1)S(1)} %copy-done.3, bf16[256,3072]{1,0:T(8,128)(2,1)S(1)} %copy-done, bf16[256,3072]{1,0:T(8,128)(2,1)S(1)} %copy-done.1, bf16[128,3072]{1,0:T(8,128)(2,1)S(1)} %copy-done.2), custom_call_target="tpu_custom_call" | custom-call | tf_op jit(solution)/shard_map/weights/pallas_call | solution.py:448
Async XLA Ops:
  52.8 1.4 %copy-start = (bf16[256,3072]{1,0:T(8,128)(2,1)S(1)}, bf16[256,3072]{1,0:T(8,128)(2,1)}, u32[]{:S(2)}) copy-start(bf16[256,3072]{1,0:T(8,128)(2,1)} %get-tuple-element.11.rows) | copy-start | bytes 4718596
  54.2 1.4 %copy-start.1 = (bf16[256,3072]{1,0:T(8,128)(2,1)S(1)}, bf16[256,3072]{1,0:T(8,128)(2,1)}, u32[]{:S(2)}) copy-start(bf16[256,3072]{1,0:T(8,128)(2,1)} %get-tuple-element.12.outs) | copy-start | bytes 4718596
  55.6 1.1 %copy-start.2 = (bf16[128,3072]{1,0:T(8,128)(2,1)S(1)}, bf16[128,3072]{1,0:T(8,128)(2,1)}, u32[]{:S(2)}) copy-start(bf16[128,3072]{1,0:T(8,128)(2,1)} %get-tuple-element.13.gin) | copy-start | bytes 2359300
  56.8 1.1 %copy-start.3 = (bf16[1536,256]{1,0:T(8,128)(2,1)S(1)}, bf16[1536,256]{1,0:T(8,128)(2,1)}, u32[]{:S(2)}) copy-start(bf16[1536,256]{1,0:T(8,128)(2,1)} %get-tuple-element.10.gt) | copy-start | bytes 2359300

commit v2 on v1

--- a/solution.py
+++ b/solution.py
@@ -173,12 +173,15 @@
         copy.start()
         return copy
 
+    def weight_rows(src, first, count):
+        return [
+            local(src.at[pl.ds(i * count, count)], wv.at[pl.ds(first + i * count, count)])
+            for i in range(src.shape[0] // count)
+        ]
+
     in_b = local(gin, tok.at[0, pl.ds(0, T)])
-    in_wd = local(wd, wv.at[pl.ds(2 * H, H)])
+    in_wd = weight_rows(wd, 2 * H, H // 4)
     in_pre = local(pre, prev)
-    in_wgu = local(wgu, wv.at[pl.ds(0, 2 * H)])
-    in_rows = local(sin, tok.at[1, pl.ds(0, T)])
-    in_outs = local(gsv, tok.at[2, pl.ds(0, T)])
 
     barrier = pltpu.get_barrier_semaphore()
     pals = [sib, ypal, xpal] + zpal[1:]
@@ -189,15 +192,17 @@
     def at_rows(a, q, h, base):
         return tok.at[a, pl.ds(pl.multiple_of(base + q * quarter + h * piece, 16), piece)]
 
-    q_me = 2 * y + c
-    q_y = 2 * (1 - y) + c
+    zbit = z % 2
+    znear = {"segment": s + 4 - 8 * zbit, "expert": x}
     arrays = (gin, sin, gsv)
     by_x, by_y, by_sib = {}, {}, {}
     for a in range(3):
+        bit, pal = (zbit, znear) if a == 1 else (y, ypal)
+        q_me, q_y = 2 * bit + c, 2 * (1 - bit) + c
         for h in range(2):
             src = arrays[a].at[pl.ds(pl.multiple_of(q_me * quarter + h * piece, 16), piece)]
             by_x[a, h] = remote(src, at_rows(a, q_me, h, T), xpal)
-            by_y[a, h] = remote(at_rows(a, q_me, h, T), at_rows(a, q_me, h, T), ypal)
+            by_y[a, h] = remote(at_rows(a, q_me, h, T), at_rows(a, q_me, h, T), pal)
             by_sib[a, h, 0] = remote(at_rows(a, q_me, h, T), at_rows(a, q_me, h, T), sib)
             by_sib[a, h, 1] = remote(at_rows(a, q_y, h, T), at_rows(a, q_y, h, T), sib)
 
@@ -205,8 +210,8 @@
         for h in range(2):
             start(by_x[a, h])
 
-    def pass_x(a):
-        for h in range(2):
+    def pass_x(a, pieces=(0, 1)):
+        for h in pieces:
             by_x[a, h].wait_recv()
             start(by_y[a, h])
             start(by_sib[a, h, 0])
@@ -231,6 +236,8 @@
     wsend[0:1, :] = share(rb, pb, 1 - x)
     wsend[1:2, :] = share(rc, pc, 1 - x)
     weights = start(remote(wsend, wrecv, xpal))
+
+    in_wgu = weight_rows(wgu, 0, H // 4)
 
     def nt(left, right):
         return lax.dot_general(left, right, (((1,), (1,)), ((), ())), preferred_element_type=F32)
@@ -261,25 +268,24 @@
     def put_keep(rows, cols, total):
         pf[rows, cols] = total
 
-    in_b.wait()
-    in_wd.wait()
-    in_pre.wait()
+    def wait_all(copies):
+        for copy in copies:
+            copy.wait()
+
+    pass_x(0, (0,))
+    wait_all([in_b, in_pre] + in_wd)
     pair_own = hidden_b(0, column(share(rb, pb, x)), x)
-    pass_x(0)
+    pass_x(0, (1,))
     send_x(1)
-    in_wgu.wait()
+    wait_all(in_wgu)
+    in_rows = local(sin, tok.at[1, pl.ds(0, T)])
+    in_outs = local(gsv, tok.at[2, pl.ds(0, T)])
     back_b(pair_own, 0, 1 - c, put_send)
     to_sib = [remote(ps.at[pl.ds(i * T, T)], pr.at[pl.ds(i * T, T)], sib) for i in range(2)]
     start(to_sib[0])
     pass_y(0)
     back_b(pair_own, 0, c, put_keep)
-    weights.wait_recv()
-    wait_sib(0)
-    pair_other = hidden_b(T, column(wrecv[0:1, :]), 1 - x)
-    back_b(pair_other, T, 1 - c, put_send)
-    start(to_sib[1])
     pass_x(1)
-    back_b(pair_other, T, c, put_keep)
 
     mine = pl.multiple_of(y * yrows, 16)
     theirs = pl.multiple_of((1 - y) * yrows, 16)
@@ -288,6 +294,13 @@
     pf[0:T, :] = pf[0:T, :] + pr[0:T, :].astype(F32)
     pm[0:T, :] = pf[0:T, :].astype(BF16)
     s2b0 = start(remote(pm.at[pl.ds(theirs, yrows), pl.ds(part, part)], r2b.at[pl.ds(0, yrows)], ypal))
+    weights.wait_recv()
+    wait_sib(0)
+    pair_other = hidden_b(T, column(wrecv[0:1, :]), 1 - x)
+    back_b(pair_other, T, 1 - c, put_send)
+    start(to_sib[1])
+    back_b(pair_other, T, c, put_keep)
+
     to_sib[1].wait_recv()
     pf[T:2 * T, :] = pf[T:2 * T, :] + pr[T:2 * T, :].astype(F32)
     pm[T:2 * T, :] = pf[T:2 * T, :].astype(BF16)
@@ -308,6 +321,7 @@
     s2b1.wait_recv()
     s3b[...] = (pf[pl.ds(T + mine, yrows), hi] + r2b[yrows:2 * yrows, :].astype(F32)).astype(BF16)
     c3b = start(remote(s3b, r3b, xpal))
+    send_x(2)
     s2b0.wait_recv()
     qf[:, lo] = pf[pl.ds(mine, yrows), lo] + r2a[pl.ds(mine, yrows), :].astype(F32)
     qf[:, hi] = pf[pl.ds(mine, yrows), hi] + r2b[0:yrows, :].astype(F32)
@@ -320,7 +334,6 @@
     for k in range(1, zn):
         there = pl.ds(pl.multiple_of(((z + k) % zn) * zrows, 16), zrows)
         z_sums.append(start(remote(qs.at[there], r4.at[k - 1], zpal[k])))
-    send_x(2)
     here = pl.multiple_of(z * zrows, 16)
     cols_me = pl.ds(pl.multiple_of(c * half, 128), half)
     chunk = qf[pl.ds(here, zrows), :] + tok[0, pl.ds(mine + here, zrows), cols_me].astype(F32)
@@ -347,7 +360,6 @@
     out_outs = local(tok.at[2], outs_o)
     scale_own = share(rc, pc, x)
     scale_c = jnp.concatenate([scale_own, wrecv[1:2, :]], axis=1)
-    gtb = gt_o
     for i in range(H // 256):
         units = slice(i * 256, i * 256 + 256)
         uppers = slice(H + i * 256, H + i * 256 + 256)
@@ -355,9 +367,9 @@
         act = nt(wv[downs, :], tok[2]) * scale_c
         upper = gt[uppers, :]
         activated, slope = silu_parts(gt[units, :])
-        gtb[units, :] = (act * upper * slope).astype(BF16)
-        gtb[uppers, :] = (act * activated).astype(BF16)
-        gtb[downs, :] = (activated * upper * scale_c).astype(BF16)
+        gt_o[units, :] = (act * upper * slope).astype(BF16)
+        gt_o[uppers, :] = (act * activated).astype(BF16)
+        gt_o[downs, :] = (activated * upper * scale_c).astype(BF16)
     for k in range(zn):
         y_out[k].wait_recv()
         sib_out.append(start(remote(finished(1 - y, k), finished(1 - y, k), sib)))
@@ -371,20 +383,45 @@
     out_go.wait()
 
 
-def weight_kernel(joined_steps, gt, rows, outs, gin, joint, last, gout):
-    i = pl.program_id(0)
-
-    @pl.when(i == 0)
-    def _():
-        gout[...] = gin[...]
-
-    @pl.when(i < joined_steps)
-    def _():
-        joint[...] = jnp.dot(gt[...], rows[...], preferred_element_type=F32).astype(BF16)
-
-    @pl.when(i >= joined_steps)
-    def _():
-        last[...] = jnp.dot(gt[...], outs[...], preferred_element_type=F32).astype(BF16)
+def weight_kernel(parts, gt, rows, outs, gin, joint, last, gout, gtv, rowv, outv, ginv, jointv, lastv, sem):
+    H, D = last.shape
+    width = D // parts
+    used = [0]
+
+    def copy(src, dst):
+        i = used[0]
+        used[0] += 1
+        made = pltpu.make_async_copy(src, dst, sem.at[i])
+        made.start()
+        return made
+
+    first = copy(gt.at[pl.ds(0, 2 * H)], gtv.at[pl.ds(0, 2 * H)])
+    spans = [pl.ds(j * width, width) for j in range(parts)]
+    in_rows = [copy(rows.at[:, span], rowv.at[:, span]) for span in spans]
+    second = copy(gt.at[pl.ds(2 * H, H)], gtv.at[pl.ds(2 * H, H)])
+    in_outs = [copy(outs.at[:, span], outv.at[:, span]) for span in spans]
+    in_gin = copy(gin, ginv)
+    done = []
+    first.wait()
+    for j in range(parts):
+        in_rows[j].wait()
+        for i in range(2):
+            units = pl.ds(i * H, H)
+            jointv[units, spans[j]] = jnp.dot(
+                gtv[units, :], rowv[:, spans[j]], preferred_element_type=F32
+            ).astype(BF16)
+            done.append(copy(jointv.at[units, spans[j]], joint.at[units, spans[j]]))
+    in_gin.wait()
+    done.append(copy(ginv, gout))
+    second.wait()
+    for j in range(parts):
+        in_outs[j].wait()
+        lastv[:, spans[j]] = jnp.dot(
+            gtv[2 * H:3 * H, :], outv[:, spans[j]], preferred_element_type=F32
+        ).astype(BF16)
+        done.append(copy(lastv.at[:, spans[j]], last.at[:, spans[j]]))
+    for made in done:
+        made.wait()
 
 
 def dense_body(
@@ -431,7 +468,7 @@
             pltpu.VMEM((2 * H, 2 * T), F32),
             pltpu.SemaphoreType.DMA((copies,)),
             pltpu.SemaphoreType.DMA((copies,)),
-            pltpu.SemaphoreType.DMA((9,)),
+            pltpu.SemaphoreType.DMA((7 + 12,)),
         ],
         compiler_params=pltpu.CompilerParams(
             collective_id=0, has_side_effects=True, vmem_limit_bytes=56 * 1024 * 1024
@@ -441,25 +478,26 @@
         grad_in, saved_in, grad_saved, route_b.T, prob_b.T, route_c.T, prob_c.T,
         pre_act.reshape(2, 2 * T, H), w_gate_up.reshape(2 * H, D), w_down.reshape(H, D),
     )
-    rows_step = 256
-    joined_steps, last_steps = 2 * H // rows_step, H // rows_step
-    whole = pl.BlockSpec((2 * T, D), lambda i: (0, 0))
-    one = pl.BlockSpec((T, D), lambda i: (0, 0))
+    parts = 6
     joint, last, grad_out = pl.pallas_call(
-        functools.partial(weight_kernel, joined_steps),
-        grid=(joined_steps + last_steps,),
+        functools.partial(weight_kernel, parts),
         out_shape=(
             jax.ShapeDtypeStruct((2 * H, D), BF16),
             jax.ShapeDtypeStruct((H, D), BF16),
             jax.ShapeDtypeStruct((T, D), BF16),
         ),
-        in_specs=[pl.BlockSpec((rows_step, 2 * T), lambda i: (i, 0)), whole, whole, one],
-        out_specs=(
-            pl.BlockSpec((rows_step, D), lambda i: (jnp.minimum(i, joined_steps - 1), 0)),
-            pl.BlockSpec((rows_step, D), lambda i: (jnp.maximum(i - joined_steps, 0), 0)),
-            one,
-        ),
-        compiler_params=pltpu.CompilerParams(vmem_limit_bytes=48 * 1024 * 1024),
+        in_specs=[hbm] * 4,
+        out_specs=(hbm,) * 3,
+        scratch_shapes=[
+            pltpu.VMEM((3 * H, 2 * T), BF16),
+            pltpu.VMEM((2 * T, D), BF16),
+            pltpu.VMEM((2 * T, D), BF16),
+            pltpu.VMEM((T, D), BF16),
+            pltpu.VMEM((2 * H, D), BF16),
+            pltpu.VMEM((H, D), BF16),
+            pltpu.SemaphoreType.DMA((5 * parts + 4,)),
+        ],
+        compiler_params=pltpu.CompilerParams(vmem_limit_bytes=63 * 1024 * 1024),
         name="weights",
     )(gt, rows, outs, gout)
     return grad_out, joint.reshape(1, 2, H, D), last.reshape(1, H, D)

time: 64.8 us -> 58 us (0.90)
  local copies, waits for them, and re-layouts: 5.07 us -> 0 us
  Pallas kernels: 58.8 us -> 56.4 us
    unnamed x8 -> x0, local copies, waits for them, and re-layouts: 5.07 us -> none
    pallas_call x1, Pallas kernels: 52.2 us -> 49.8 us  [dense_body(): pl.pallas_call(functools.partial(exchange_kernel, zn), out_shape=(jax.Sha...]
where the time goes in v2:
time: 58 us; the launch traced here: 57.1 us
  Pallas kernels  56.4 us (97%)
  between operations  0.64 us (1%)
    pallas_call x1, Pallas kernels, dense_body(): pl.pallas_call(functools.partial(exchange_kernel, zn), out_shape=(jax.Sha...  49.8 us
    pallas_call x1, Pallas kernels, dense_body(): pl.pallas_call(functools.partial(weight_kernel, parts), out_shape=(jax.Sh...  6.63 us

profile of v2, /device:TPU:0, one launch (start us, length us, event | category | flops | bytes accessed | tf_op | source)
XLA Modules:
  0.0 57.1 jit_solution(6552998745269314971)
XLA Ops:
  0.6 49.8 %exchange.1 = (bf16[128,3072]{1,0:T(8,128)(2,1)}, bf16[256,3072]{1,0:T(8,128)(2,1)}, bf16[256,3072]{1,0:T(8,128)(2,1)}, bf16[1536,256]{1,0:T(8,128)(2,1)}) custom-call(bf16[128,3072]{1,0:T(8,128)(2,1)} %gin.1, bf16[128,3072]{1,0:T(8,128)(2,1)} %sin.1, bf16[128,3072]{1,0:T(8,128)(2,1)} %gsv.1, s32[2,128]{1,0:T(2,128)} %bitcast.12, f32[2,128]{1,0:T(2,128)} %bitcast.13, ...), custom_call_target="tpu_custom_call" | custom-call | tf_op jit(solution)/shard_map/exchange/pallas_call | solution.py:438
  50.5 6.6 %weights.1 = (bf16[1024,3072]{1,0:T(8,128)(2,1)}, bf16[512,3072]{1,0:T(8,128)(2,1)}, bf16[128,3072]{1,0:T(8,128)(2,1)}) custom-call(bf16[1536,256]{1,0:T(8,128)(2,1)} %get-tuple-element.10.gt, bf16[256,3072]{1,0:T(8,128)(2,1)} %get-tuple-element.11.rows, bf16[256,3072]{1,0:T(8,128)(2,1)} %get-tuple-element.12.outs, bf16[128,3072]{1,0:T(8,128)(2,1)} %get-tuple-element.13.gin), custom_call_target="tpu_custom_call" | custom-call | tf_op jit(solution)/shard_map/weights/pallas_call | solution.py:482
